TPU v7x, 256 devices: a whole 4x4x8 slice. The times are simulated.
256 devices in a mesh: blk: 64 (over x, z, core), rep: 4 (over y).
Axes of the slice: x: 4, y: 4, z: 8, core: 2. Of those that a mesh axis runs over, the one named last changes fastest.
Arguments:
- right_side: float32 [64, 262144], P(None, 'blk'), may hold values from -6 to 6
- points: float32 [3, 262144], P(None, 'blk'), may hold values from -1 to 544, as said below
- active: int32 [64, 5], replicated, may hold values 0 or 1
Outputs:
- posterior_mean: float32 [64, 262144], P(None, 'blk')
- residual: float32 [64, 262144], P(None, 'blk')
Inputs may be any that keep to these rules, and one draw needn't show every extreme that they name: `points`: point coordinates in lattice units.
All inputs are finite; a program needn't handle non-finite values.
Results may differ from a plain program's by a relative error of at most 0.0003.
Values sent between devices are 32-bit elements; how exact they have to be, the bound alone decides.
No kernel may reach another device: no remote copies, remote signals or barrier semaphores. Data moves between devices by JAX's collectives and lax.ppermute only.
A program may use at most 128 MiB of HBM per device.

v0:
```python
from functools import partial
import jax
import jax.numpy as jnp
from jax import lax
from jax.sharding import PartitionSpec as P

ITERS = 2
B = 2048
support_radius = 2.5
noise_level = 8.0


def from_behind(block, axis, distance):
    devices = range(lax.axis_size(axis))
    route = [(i - distance, i) for i in devices if i - distance in devices]
    return lax.ppermute(block, axis, route)


def wendland(rows, cols):
    delta_x = rows[0][:, None] - cols[0][None, :]
    delta_y = rows[1][:, None] - cols[1][None, :]
    delta_z = rows[2][:, None] - cols[2][None, :]
    scaled = jnp.sqrt(delta_x * delta_x + delta_y * delta_y + delta_z * delta_z) / support_radius
    inside = jnp.maximum(1.0 - scaled, 0.0)
    square = inside * inside
    return square * square * (4.0 * scaled + 1.0)


def apply_rows(vector, kernel_tile):
    return lax.dot_general(
        vector,
        kernel_tile,
        (((1,), (1,)), ((), ())),
        precision=lax.Precision.HIGHEST,
        preferred_element_type=jnp.float32,
    )


def apply_cols(vector, kernel_tile):
    return jnp.dot(
        vector, kernel_tile, precision=lax.Precision.HIGHEST, preferred_element_type=jnp.float32
    )


def pair_flags(active, column, count):
    here = lax.dynamic_slice_in_dim(active, column, 1, 0)[0].astype(jnp.float32)
    before = lax.dynamic_slice_in_dim(active, jnp.maximum(column - 1, 0), 1, 0)[0].astype(
        jnp.float32
    )
    has_before = (column >= 1).astype(jnp.float32)
    has_after = (column + 1 < count).astype(jnp.float32)
    table = []
    for c in range(2):
        entry = []
        for k in range(6):
            if k < 2:
                entry.append(before[1 + 2 * k + c] * has_before)
            elif k == 2 + c:
                entry.append(has_after * 0.0 + 1.0)
            elif k < 4:
                entry.append(here[0])
            else:
                entry.append(here[1 + 2 * c + (k - 4)] * has_after)
        table.append(entry)
    return table


def gated(flag, compute, operands):
    return flag * compute(*operands)


def place_rows(values, start, total):
    return lax.dynamic_update_slice_in_dim(
        jnp.zeros((values.shape[0], total), jnp.float32), values, start, 1
    )


def shards(right_side, points, active):
    count = lax.axis_size("blk")
    column = lax.axis_index("blk")
    groups = lax.axis_size("rep")
    member = lax.axis_index("rep")
    flags = pair_flags(active, column, count)
    rows_each = B // groups
    row_start = member * rows_each
    sides = right_side.shape[0]

    def row_slice(array, c):
        return lax.dynamic_slice_in_dim(array, c * B + row_start, rows_each, 1)

    def fetch(stored, index):
        return stored[index]

    pts_next = from_behind(points, "blk", -1)
    makers = [
        partial(wendland, row_slice(points, c), points[:, c * B : (c + 1) * B]) for c in range(2)
    ]
    makers.append(partial(wendland, row_slice(points, 0), points[:, B : 2 * B]))
    for c in range(2):
        for k in range(2):
            makers.append(partial(wendland, row_slice(points, c), pts_next[:, k * B : (k + 1) * B]))
    stored = [maker() for maker in makers]

    def matvec(vector):
        vec_next = from_behind(vector, "blk", -1)
        own_rows = [row_slice(vector, c) for c in range(2)]
        row_terms = [apply_rows(vector[:, c * B : (c + 1) * B], fetch(stored, c)) for c in range(2)]
        across_tile = fetch(stored, 2)
        row_terms[0] = row_terms[0] + gated(
            flags[0][3], apply_rows, (vector[:, B : 2 * B], across_tile)
        )
        across_back = gated(flags[0][3], apply_cols, (own_rows[0], across_tile))
        next_terms = [jnp.zeros((sides, B), jnp.float32), jnp.zeros((sides, B), jnp.float32)]
        for c in range(2):
            for k in range(2):
                kernel_tile = fetch(stored, 3 + 2 * c + k)
                flag = flags[c][4 + k]
                row_terms[c] = row_terms[c] + gated(
                    flag, apply_rows, (vec_next[:, k * B : (k + 1) * B], kernel_tile)
                )
                next_terms[k] = next_terms[k] + gated(flag, apply_cols, (own_rows[c], kernel_tile))
        own_full = jnp.concatenate(
            [
                place_rows(row_terms[0], row_start, B),
                across_back + place_rows(row_terms[1], row_start, B),
            ],
            axis=1,
        )
        returned = from_behind(jnp.concatenate(next_terms, axis=1), "blk", 1)
        total = lax.psum(own_full + returned, "rep")
        return total + noise_level * vector

    def squares(residual):
        return lax.psum(jnp.sum(residual * residual, axis=1), "blk")

    solution = jnp.zeros_like(right_side)
    residual = right_side
    direction = right_side
    norm_now = squares(residual)
    for step in range(ITERS):
        image = matvec(direction)
        alpha = norm_now / lax.psum(jnp.sum(direction * image, axis=1), "blk")
        solution = solution + alpha[:, None] * direction
        residual = residual - alpha[:, None] * image
        norm_next = squares(residual)
        direction = residual + (norm_next / norm_now)[:, None] * direction
        norm_now = norm_next
    posterior = right_side - noise_level * solution
    return (posterior, residual)


def solution(mesh):
    return jax.shard_map(
        shards,
        mesh=mesh,
        in_specs=(P(None, "blk"), P(None, "blk"), P()),
        out_specs=(P(None, "blk"), P(None, "blk")),
        check_vma=False,
    )
```

profile of v0, /device:TPU:8, one launch (start us, length us, event | category | flops | bytes accessed | tf_op | source)
XLA Modules:
  0.0 681.2 jit_solution(9274392147604572619)
XLA Ops:
  13.1 8.3 %fusion.17 = f32[512,64]{0,1:T(8,128)S(1)} fusion(f32[512]{0:T(512)S(1)} %bitcast.125, f32[512]{0:T(512)S(1)} %bitcast.115, f32[512]{0:T(512)S(1)} %bitcast.105, f32[2048]{0:T(1024)S(1)} %bitcast.39, f32[2048]{0:T(1024)S(1)} %bitcast.45, f32[2048]{0:T(1024)S(1)} %bitcast.51, f32[64,4096]{1,0:T(8,128)} %param.3), kind=kOutput, calls=%fused_computation.34 | convolution fusion | flops 822083584 | bytes 686080 | tf_op jit(solution)/shard_map/dot_general | solution.py:30
  21.4 8.1 %fusion.44 = f32[512,64]{0,1:T(8,128)S(1)} fusion(f32[2048]{0:T(1024)S(1)} %bitcast.40, f32[2048]{0:T(1024)S(1)} %bitcast.46, f32[2048]{0:T(1024)S(1)} %bitcast.52, f32[512]{0:T(512)S(1)} %bitcast.163, f32[512]{0:T(512)S(1)} %bitcast.135, f32[512]{0:T(512)S(1)} %bitcast.149, f32[64,4096]{1,0:T(8,128)S(1)} %copy-done, f32[]{:T(128)} %bitcast.6), kind=kOutput, calls=%fused_computation.61 | convolution fusion | flops 822116352 | bytes 686084 | tf_op jit(solution)/shard_map/dot_general | solution.py:30
  29.5 7.2 %fusion.18 = f32[512,64]{0,1:T(8,128)S(1)} fusion(f32[512,64]{0,1:T(8,128)S(1)} %fusion.44, f32[2048]{0:T(1024)S(1)} %bitcast.35, f32[512]{0:T(512)S(1)} %bitcast.164, f32[2048]{0:T(1024)S(1)} %bitcast.37, f32[512]{0:T(512)S(1)} %bitcast.136, f32[2048]{0:T(1024)S(1)} %bitcast.33, f32[512]{0:T(512)S(1)} %bitcast.150, f32[64,4096]{1,0:T(8,128)S(1)} %copy-done), kind=kOutput, calls=%fused_computation.35 | convolution fusion | flops 822116352 | bytes 817152 | tf_op jit(solution)/shard_map/dot_general | solution.py:30
  36.7 6.6 convolution_multiply_fusion.9
  45.8 5.7 convolution_multiply_fusion.8
  51.6 5.7 fusion.3
  57.3 5.9 convolution_multiply_fusion.6
  63.3 5.7 fusion.2
  69.1 4.1 collective-permute-start.2
  73.2 7.2 %fusion.41 = f32[512,64]{0,1:T(8,128)S(1)} fusion(f32[512,64]{0,1:T(8,128)S(1)} %fusion.18, f32[2048]{0:T(1024)S(1)} %bitcast.91, f32[2048]{0:T(1024)S(1)} %bitcast.99, f32[2048]{0:T(1024)S(1)} %bitcast.83, f32[512]{0:T(512)S(1)} %bitcast.168, f32[512]{0:T(512)S(1)} %bitcast.140, f32[512]{0:T(512)S(1)} %bitcast.154, ...), kind=kOutput, calls=%fused_computation.58 | convolution fusion | flops 822149120 | bytes 817156 | tf_op jit(solution)/shard_map/dot_general | solution.py:30
  80.4 7.3 %fusion.36 = f32[64,2048]{1,0:T(8,128)S(1)} fusion(f32[64,2048]{1,0:T(8,128)S(1)} %broadcast.47.clone, s32[]{:T(128)S(6)} %select_n.10, f32[512,64]{0,1:T(8,128)S(1)} %fusion.41, f32[2048]{0:T(1024)S(1)} %bitcast.59, f32[2048]{0:T(1024)S(1)} %bitcast.67, f32[2048]{0:T(1024)S(1)} %bitcast.75, f32[512]{0:T(512)S(1)} %bitcast.169, f32[512]{0:T(512)S(1)} %bitcast.141, ...), kind=kOutput, calls=%fused_computation.53 | convolution fusion | flops 822149120 | bytes 817160 | tf_op jit(solution)/shard_map/dot_general | solution.py:30
  87.8 7.2 %fusion.30 = f32[512,64]{0,1:T(8,128)S(1)} fusion(f32[512,64]{0,1:T(8,128)S(1)} %fusion.17, f32[512]{0:T(512)S(1)} %bitcast.128, f32[512]{0:T(512)S(1)} %bitcast.118, f32[512]{0:T(512)S(1)} %bitcast.108, f32[2048]{0:T(1024)S(1)} %bitcast.92, f32[2048]{0:T(1024)S(1)} %bitcast.100, f32[2048]{0:T(1024)S(1)} %bitcast.84, ...), kind=kOutput, calls=%fused_computation.47 | convolution fusion | flops 822149120 | bytes 817156 | tf_op jit(solution)/shard_map/dot_general | solution.py:30
  95.0 7.4 %fusion.24 = f32[64,2048]{1,0:T(8,128)S(1)} fusion(f32[64,2048]{1,0:T(8,128)S(1)} %convolution_multiply_fusion.9, s32[]{:T(128)S(6)} %select_n.10, f32[512,64]{0,1:T(8,128)S(1)} %fusion.30, f32[512]{0:T(512)S(1)} %bitcast.129, f32[512]{0:T(512)S(1)} %bitcast.119, f32[512]{0:T(512)S(1)} %bitcast.109, f32[2048]{0:T(1024)S(1)} %bitcast.60, ...), kind=kOutput, calls=%fused_computation.41 | convolution fusion | flops 822181888 | bytes 948232 | tf_op jit(solution)/shard_map/dot_general | solution.py:30
  103.5 55.2 %all-reduce.4.cloned.1.call-done = f32[64,4096]{1,0:T(8,128)} async-done(((f32[64,4096]{1,0:T(8,128)}), f32[64,4096]{1,0:T(8,128)}) %all-reduce.4.cloned.1.call-update) | async-done | bytes 1048592 | tf_op jit(solution)/shard_map/psum | solution.py:130
  160.4 127.9 %all-reduce = (f32[64]{0:T(128)S(1)}, f32[64]{0:T(128)S(1)}) all-reduce(f32[64]{0:T(128)S(1)} %get-tuple-element.3, f32[64]{0:T(128)S(1)} %get-tuple-element.2), channel_id=1, replica_groups=mesh['blk'=64,'rep'=4] {'blk'}, use_global_device_ids=true, to_apply=%region_1.0 | all-reduce | flops 128 | bytes 1024 | tf_op jit(solution)/shard_map/psum | solution.py:134
  288.6 124.1 %psum.45 = f32[64]{0:T(128)S(1)} all-reduce(f32[64]{0:T(128)S(1)} %multiply_reduce_fusion.1), channel_id=1, replica_groups=mesh['blk'=64,'rep'=4] {'blk'}, use_global_device_ids=true, to_apply=%region_6.0 | all-reduce | flops 64 | bytes 512 | tf_op jit(solution)/shard_map/psum | solution.py:134
  412.9 7.4 %fusion.45 = f32[64,512]{1,0:T(8,128)S(1)} fusion(f32[2048]{0:T(1024)S(1)} %bitcast.42, f32[2048]{0:T(1024)S(1)} %bitcast.48, f32[2048]{0:T(1024)S(1)} %bitcast.54, f32[512]{0:T(512)S(1)} %bitcast.170, f32[512]{0:T(512)S(1)} %bitcast.142, f32[512]{0:T(512)S(1)} %bitcast.156, f32[64,4096]{1,0:T(8,128)S(1)} %multiply_add_fusion.1, f32[]{:T(128)} %bitcast.6), kind=kOutput, calls=%fused_computation.62 | convolution fusion | flops 822116352 | bytes 686084 | tf_op jit(solution)/shard_map/dot_general | solution.py:30
  422.0 6.7 fusion.16
  428.8 5.7 convolution_multiply_fusion.3
  434.5 5.9 convolution_multiply_fusion.1
  440.4 5.7 fusion.1
  446.2 6.1 fusion
  452.4 3.1 collective-permute-start.4
  455.5 6.4 convolution_multiply_fusion.4
  461.9 6.7 fusion.19
  468.7 6.9 %fusion.43 = f32[64,512]{1,0:T(8,128)S(1)} fusion(f32[64,512]{1,0:T(8,128)S(1)} %fusion.19, f32[2048]{0:T(1024)S(1)} %bitcast.95, f32[2048]{0:T(1024)S(1)} %bitcast.103, f32[2048]{0:T(1024)S(1)} %bitcast.87, f32[512]{0:T(512)S(1)} %bitcast.175, f32[512]{0:T(512)S(1)} %bitcast.147, f32[512]{0:T(512)S(1)} %bitcast.161, ...), kind=kOutput, calls=%fused_computation.60 | convolution fusion | flops 822149120 | bytes 817156 | tf_op jit(solution)/shard_map/dot_general | solution.py:30
  475.6 6.8 fusion.39
  482.4 7.0 %fusion.32 = f32[64,512]{1,0:T(8,128)S(1)} fusion(f32[64,512]{1,0:T(8,128)S(1)} %fusion.16, f32[512]{0:T(512)S(1)} %bitcast.133, f32[512]{0:T(512)S(1)} %bitcast.123, f32[512]{0:T(512)S(1)} %bitcast.113, f32[2048]{0:T(1024)S(1)} %bitcast.96, f32[2048]{0:T(1024)S(1)} %bitcast.104, f32[2048]{0:T(1024)S(1)} %bitcast.88, ...), kind=kOutput, calls=%fused_computation.49 | convolution fusion | flops 822149120 | bytes 817156 | tf_op jit(solution)/shard_map/dot_general | solution.py:30
  489.3 6.8 fusion.28
  497.2 44.3 %all-reduce.6.cloned.1.call-done = f32[64,4096]{1,0:T(8,128)} async-done(((f32[64,4096]{1,0:T(8,128)}), f32[64,4096]{1,0:T(8,128)}) %all-reduce.6.cloned.1.call-update) | async-done | bytes 1048592 | tf_op jit(solution)/shard_map/psum | solution.py:130
  543.0 127.9 %psum.47 = f32[64]{0:T(128)S(1)} all-reduce(f32[64]{0:T(128)S(1)} %multiply_reduce_fusion), channel_id=1, replica_groups=mesh['blk'=64,'rep'=4] {'blk'}, use_global_device_ids=true, to_apply=%region_9.0 | all-reduce | flops 64 | bytes 512 | tf_op jit(solution)/shard_map/psum | solution.py:142
  670.9 3.0 multiply_subtract_fusion
  (34 shorter events, 13.8 us)
Async XLA Ops:
  7.2 151.6 %all-reduce.4.cloned.1.call-start = ((), (), s32[]{:S(2)}) async-start(), calls=%async_computation | async-start | bytes 2097152 | tf_op jit(solution)/shard_map/psum | solution.py:130
  7.2 38.5 %collective-permute-start = (f32[3,4096]{1,0:T(4,128)}, f32[3,4096]{1,0:T(4,128)S(1)}, u32[]{:S(2)}, u32[]{:S(2)}) collective-permute-start(f32[3,4096]{1,0:T(4,128)} %param.4), channel_id=1, source_target_pairs={{4,0},{8,4},{12,8},{16,12},{20,16},{24,20},{28,24},{32,28},{36,32}... | collective-permute-start | bytes 147464 | tf_op jit(solution)/shard_map/ppermute | solution.py:16
  8.5 64.7 %collective-permute-start.1 = (f32[64,4096]{1,0:T(8,128)}, f32[64,4096]{1,0:T(8,128)S(1)}, u32[]{:S(2)}, u32[]{:S(2)}) collective-permute-start(f32[64,4096]{1,0:T(8,128)} %param.3), channel_id=1, source_target_pairs={{4,0},{8,4},{12,8},{16,12},{20,16},{24,20},{28,24},{32,28},{36,32}... | collective-permute-start | bytes 3145736 | tf_op jit(solution)/shard_map/ppermute | solution.py:16
  13.1 8.3 %copy-start = (f32[64,4096]{1,0:T(8,128)S(1)}, f32[64,4096]{1,0:T(8,128)}, u32[]{:S(2)}) copy-start(f32[64,4096]{1,0:T(8,128)} %param.3) | copy-start | bytes 3145732
  69.1 33.2 %collective-permute-start.2 = (f32[64,4096]{1,0:T(8,128)S(1)}, f32[64,4096]{1,0:T(8,128)S(1)}, u32[]{:S(2)}, u32[]{:S(2)}) collective-permute-start(f32[64,4096]{1,0:T(8,128)S(1)} %pad_maximum_fusion), channel_id=1, source_target_pairs={{0,4},{4,8},{8,12},{12,16},{16,20},{20,24},{24,28},{28,32},{32,36}... | collective-permute-start | bytes 3145736 | tf_op jit(solution)/shard_map/ppermute | solution.py:16
  103.5 438.1 %all-reduce.6.cloned.1.call-start = ((), (), s32[]{:S(2)}) async-start(), calls=%async_computation.1 | async-start | bytes 2097152 | tf_op jit(solution)/shard_map/psum | solution.py:130
  158.7 129.5 %copy-start.1 = (f32[64,4096]{1,0:T(8,128)S(1)}, f32[64,4096]{1,0:T(8,128)}, u32[]{:S(2)}) copy-start(f32[64,4096]{1,0:T(8,128)} %all-reduce.4.cloned.1.call-done) | copy-start | bytes 3145732
  420.3 48.3 %collective-permute-start.3 = (f32[64,4096]{1,0:T(8,128)S(1)}, f32[64,4096]{1,0:T(8,128)S(1)}, u32[]{:S(2)}, u32[]{:S(2)}) collective-permute-start(f32[64,4096]{1,0:T(8,128)S(1)} %multiply_add_fusion.1), channel_id=1, source_target_pairs={{4,0},{8,4},{12,8},{16,12},{20,16},{24,20},{28,24},{32,28},{36,32}... | collective-permute-start | bytes 3145736 | tf_op jit(solution)/shard_map/ppermute | solution.py:16
  452.4 43.7 %collective-permute-start.4 = (f32[64,4096]{1,0:T(8,128)S(1)}, f32[64,4096]{1,0:T(8,128)S(1)}, u32[]{:S(2)}, u32[]{:S(2)}) collective-permute-start(f32[64,4096]{1,0:T(8,128)S(1)} %pad_maximum_fusion.1), channel_id=1, source_target_pairs={{0,4},{4,8},{8,12},{12,16},{16,20},{20,24},{24,28},{28,32},{32,36}... | collective-permute-start | bytes 3145736 | tf_op jit(solution)/shard_map/ppermute | solution.py:16
Sparse Core Ops, SparseCore 0:
  103.6 55.1 all-reduce.3
  497.3 44.1 all-reduce.5
where the time goes:
time: 690 us; the launch traced here: 681 us
  blocking collectives  380 us (55%)
  matrix products  161 us (23%)
  waiting for transfers between devices  99.6 us (14%)
  between operations  17.2 us (2%)
  starting transfers between devices  11.6 us (2%)
  other arithmetic  9.81 us (1%)
    psum x2, blocking collectives, squares(): return lax.psum(jnp.sum(residual * residual, axis=1), 'blk')  252 us
    psum x1, blocking collectives, shards(): alpha = norm_now / lax.psum(jnp.sum(direction * image, axis=1), 'blk')  128 us
    dot_general x14, matrix products, apply_rows(): lax.dot_general(vector, kernel_tile, (((1,), (1,)), ((), ())), precision=...  101 us
    psum x2, waiting for transfers between devices, matvec(): total = lax.psum(own_full + returned, 'rep')  99.6 us
    dot_general x10, matrix products, apply_cols(): jnp.dot(vector, kernel_tile, precision=lax.Precision.HIGHEST, preferred_e...  59.7 us
  transfers between devices with their start and end apart: 7, of which 2 were waited for; matrix products, arithmetic and copies ran while one was open for 23% of the time, Pallas kernels for 0%

commit v1 on v0

--- a/solution.py
+++ b/solution.py
@@ -139,7 +139,9 @@
     norm_now = squares(residual)
     for step in range(ITERS):
         image = matvec(direction)
-        alpha = norm_now / lax.psum(jnp.sum(direction * image, axis=1), "blk")
+        alpha = norm_now / jnp.sum(
+            lax.all_gather(jnp.sum(direction * image, axis=1), "blk"), axis=0
+        )
         solution = solution + alpha[:, None] * direction
         residual = residual - alpha[:, None] * image
         norm_next = squares(residual)

time: 690 us -> 935 us (1.36)
  blocking collectives: 380 us -> 624 us
    unnamed x0 -> x1, blocking collectives: none -> 250 us
    psum x1 -> x0, blocking collectives: 128 us -> none  [shards(): alpha = norm_now / lax.psum(jnp.sum(direction * image, axis=1), 'blk')]
    psum x2, blocking collectives: 252 us -> 374 us  [squares(): return lax.psum(jnp.sum(residual * residual, axis=1), 'blk')]
  transfers between devices with their start and end apart: 7 -> 7, of which waited for: 2 -> 2; matrix products, arithmetic and copies ran while one was open for 23% -> 17% of each run, Pallas kernels for 0% -> 0%
where the time goes in v1:
time: 935 us; the launch traced here: 926 us
  blocking collectives  624 us (67%)
  matrix products  161 us (17%)
  waiting for transfers between devices  97.7 us (10%)
  between operations  17.9 us (2%)
  starting transfers between devices  11.6 us (1%)
  other arithmetic  9.88 us (1%)
    psum x2, blocking collectives, squares(): return lax.psum(jnp.sum(residual * residual, axis=1), 'blk')  374 us
    unnamed x1, blocking collectives  250 us
    dot_general x14, matrix products, apply_rows(): lax.dot_general(vector, kernel_tile, (((1,), (1,)), ((), ())), precision=...  101 us
    psum x2, waiting for transfers between devices, matvec(): total = lax.psum(own_full + returned, 'rep')  97.6 us
    dot_general x10, matrix products, apply_cols(): jnp.dot(vector, kernel_tile, precision=lax.Precision.HIGHEST, preferred_e...  59.7 us
  transfers between devices with their start and end apart: 7, of which 2 were waited for; matrix products, arithmetic and copies ran while one was open for 17% of the time, Pallas kernels for 0%

profile of v1, /device:TPU:8, one launch (start us, length us, event | category | flops | bytes accessed | tf_op | source)
XLA Modules:
  0.0 926.0 jit_solution(11297758279202484339)
XLA Ops:
  13.1 8.3 fusion.17
  21.4 8.1 fusion.44
  29.5 7.2 fusion.18
  36.7 6.6 convolution_multiply_fusion.9
  45.8 5.7 convolution_multiply_fusion.8
  51.6 5.7 fusion.3
  57.3 5.9 convolution_multiply_fusion.6
  63.3 5.7 fusion.2
  69.1 4.1 collective-permute-start.2
  73.2 7.2 fusion.41
  80.4 7.3 fusion.36
  87.8 7.2 fusion.30
  94.9 7.4 fusion.24
  105.5 53.2 %all-reduce.6.cloned.1.call-done = f32[64,4096]{1,0:T(8,128)} async-done(((f32[64,4096]{1,0:T(8,128)}), f32[64,4096]{1,0:T(8,128)}) %all-reduce.6.cloned.1.call-update) | async-done | bytes 1048592 | tf_op jit(solution)/shard_map/psum | solution.py:130
  160.6 249.9 %all-reduce.2 = (f32[64]{0:T(128)S(1)}, f32[4096]{0:T(1024)S(1)}) all-reduce(f32[64]{0:T(128)S(1)} %get-tuple-element.3, f32[4096]{0:T(1024)S(1)} %dynamic-update-slice.2), channel_id=1, replica_groups=mesh['blk'=64,'rep'=4] {'blk'}, use_global_device_ids=true, to_apply=%region_1.0 | all-reduce | flops 4160 | bytes 33280 | tf_op jit(solution)/shard_map/psum | solution.py:134
  411.0 124.0 %psum.30 = f32[64]{0:T(128)S(1)} all-reduce(f32[64]{0:T(128)S(1)} %multiply_reduce_fusion.1), channel_id=1, replica_groups=mesh['blk'=64,'rep'=4] {'blk'}, use_global_device_ids=true, to_apply=%region_6.0 | all-reduce | flops 64 | bytes 512 | tf_op jit(solution)/shard_map/psum | solution.py:134
  535.3 7.4 fusion.45
  544.4 6.7 fusion.16
  551.2 5.7 convolution_multiply_fusion.3
  556.9 5.9 convolution_multiply_fusion.1
  562.8 5.7 fusion.1
  568.6 6.1 fusion
  574.8 3.1 collective-permute-start.4
  577.9 6.4 convolution_multiply_fusion.4
  584.3 6.7 fusion.19
  591.1 6.9 fusion.43
  598.0 6.8 fusion.39
  604.8 7.0 fusion.32
  611.8 6.8 fusion.28
  619.6 44.4 %all-reduce.8.cloned.1.call-done = f32[64,4096]{1,0:T(8,128)} async-done(((f32[64,4096]{1,0:T(8,128)}), f32[64,4096]{1,0:T(8,128)}) %all-reduce.8.cloned.1.call-update) | async-done | bytes 1048592 | tf_op jit(solution)/shard_map/psum | solution.py:130
  665.8 249.9 %all-reduce.1 = f32[4096]{0:T(1024)S(1)} all-reduce(f32[4096]{0:T(1024)S(1)} %dynamic-update-slice.3), channel_id=3, replica_groups=mesh['blk'=64,'rep'=4] {'blk'}, use_global_device_ids=true, to_apply=%add.1 | all-reduce | flops 4096 | bytes 32768
  915.8 3.0 multiply_subtract_fusion
  (45 shorter events, 15.8 us)
Async XLA Ops:
  7.2 151.6 %all-reduce.6.cloned.1.call-start = ((), (), s32[]{:S(2)}) async-start(), calls=%async_computation | async-start | bytes 2097152 | tf_op jit(solution)/shard_map/psum | solution.py:130
  7.2 38.5 %collective-permute-start = (f32[3,4096]{1,0:T(4,128)}, f32[3,4096]{1,0:T(4,128)S(1)}, u32[]{:S(2)}, u32[]{:S(2)}) collective-permute-start(f32[3,4096]{1,0:T(4,128)} %param.4), channel_id=1, source_target_pairs={{4,0},{8,4},{12,8},{16,12},{20,16},{24,20},{28,24},{32,28},{36,32}... | collective-permute-start | bytes 147464 | tf_op jit(solution)/shard_map/ppermute | solution.py:16
  8.5 64.7 %collective-permute-start.1 = (f32[64,4096]{1,0:T(8,128)}, f32[64,4096]{1,0:T(8,128)S(1)}, u32[]{:S(2)}, u32[]{:S(2)}) collective-permute-start(f32[64,4096]{1,0:T(8,128)} %param.3), channel_id=1, source_target_pairs={{4,0},{8,4},{12,8},{16,12},{20,16},{24,20},{28,24},{32,28},{36,32}... | collective-permute-start | bytes 3145736 | tf_op jit(solution)/shard_map/ppermute | solution.py:16
  13.1 8.3 copy-start
  69.1 33.2 %collective-permute-start.2 = (f32[64,4096]{1,0:T(8,128)S(1)}, f32[64,4096]{1,0:T(8,128)S(1)}, u32[]{:S(2)}, u32[]{:S(2)}) collective-permute-start(f32[64,4096]{1,0:T(8,128)S(1)} %pad_maximum_fusion), channel_id=1, source_target_pairs={{0,4},{4,8},{8,12},{12,16},{16,20},{20,24},{24,28},{28,32},{32,36}... | collective-permute-start | bytes 3145736 | tf_op jit(solution)/shard_map/ppermute | solution.py:16
  103.4 0.7 copy-start.2
  103.5 560.5 %all-reduce.8.cloned.1.call-start = ((), (), s32[]{:S(2)}) async-start(), calls=%async_computation.1 | async-start | bytes 2097152 | tf_op jit(solution)/shard_map/psum | solution.py:130
  158.7 252.0 %copy-start.1 = (f32[64,4096]{1,0:T(8,128)S(1)}, f32[64,4096]{1,0:T(8,128)}, u32[]{:S(2)}) copy-start(f32[64,4096]{1,0:T(8,128)} %all-reduce.6.cloned.1.call-done) | copy-start | bytes 3145732
  542.7 48.3 %collective-permute-start.3 = (f32[64,4096]{1,0:T(8,128)S(1)}, f32[64,4096]{1,0:T(8,128)S(1)}, u32[]{:S(2)}, u32[]{:S(2)}) collective-permute-start(f32[64,4096]{1,0:T(8,128)S(1)} %multiply_add_fusion.1), channel_id=1, source_target_pairs={{4,0},{8,4},{12,8},{16,12},{20,16},{24,20},{28,24},{32,28},{36,32}... | collective-permute-start | bytes 3145736 | tf_op jit(solution)/shard_map/ppermute | solution.py:16
  574.8 43.7 %collective-permute-start.4 = (f32[64,4096]{1,0:T(8,128)S(1)}, f32[64,4096]{1,0:T(8,128)S(1)}, u32[]{:S(2)}, u32[]{:S(2)}) collective-permute-start(f32[64,4096]{1,0:T(8,128)S(1)} %pad_maximum_fusion.1), channel_id=1, source_target_pairs={{0,4},{4,8},{8,12},{12,16},{16,20},{20,24},{24,28},{28,32},{32,36}... | collective-permute-start | bytes 3145736 | tf_op jit(solution)/shard_map/ppermute | solution.py:16
Sparse Core Ops, SparseCore 0:
  103.6 55.0 all-reduce.5
  619.8 44.1 all-reduce.7
